TPU v7x, 512 devices: a whole 4x8x8 slice. The times are simulated.
512 devices in a mesh: pool: 32 (over z, y_hi, core), tp: 16 (over x, y_lo).
Axes of the slice: x: 4, y: 8 (y_hi: 2, y_lo: 4; y = y_hi * 4 + y_lo), z: 8, core: 2. Of those that a mesh axis runs over, the one named last changes fastest.
Arguments:
- turn_query_rows: bfloat16 [8192, 8192], P('pool', 'tp'), may hold values from -40 to 40
- turn_key_value: bfloat16 [32, 2, 256, 1024], P('pool', None, 'tp'), may hold values from -40 to 40
- prefix_page_store: bfloat16 [1024, 2, 64, 1024], P('pool', None, 'tp'), may hold values from -6 to 6
- prefix_pages: int32 [32], replicated, may hold values from 16 to 32
- holder_table: int32 [32, 32], replicated, may hold values from 0 to 31, as said below
- out_weight: bfloat16 [8192, 4096], P('tp', 'pool'), may hold values from -0.0625 to 0.0625
- row_request: int32 [256], replicated, may hold values from 0 to 31
- step_query: bfloat16 [2, 256, 8192], P(None, 'pool', 'tp'), may hold values from -40 to 40
- step_kv: bfloat16 [2, 256, 2, 1024], P(None, 'pool'), may hold values from -40 to 40
Outputs:
- prefill_out: bfloat16 [8192, 4096], P(('pool', 'tp'))
- decode_out: bfloat16 [2, 256, 8192], P(None, 'pool', 'tp')
- decode_cache: bfloat16 [32, 32, 2, 2, 64, 1024], P('pool', None, None, None, None, 'tp')
Inputs may be any that keep to these rules, and one draw needn't show every extreme that they name: `holder_table`: the pages of each request form 1 aligned blocks of 32 consecutive pages; the pages of one block lie on 32 distinct holders.
All inputs are finite; a program needn't handle non-finite values.
Results may differ from a plain program's by a relative error of at most 0.024.
Values may be sent and summed in bfloat16 or wider, within the bound.
A program may use at most 128 MiB of HBM per device.

v0:
```python
import math

import jax
import jax.numpy as jnp
import numpy as np
from jax import lax
from jax.sharding import PartitionSpec as P

QUERY_HEADS = 64
KEY_VALUE_HEADS = 8
HEAD_SIZE = 128
PAGE_POSITIONS = 64
PREFIX_PAGE_CAP = 32
TURN_TOKENS = 256
DECODE_STEPS = 2


def head_columns(tensor_split_count, heads_dev, group_width, kv_dev):
    target = np.arange(tensor_split_count)[:, None]
    local_head = np.arange(kv_dev)[None, :]
    return (target * heads_dev // group_width + local_head).reshape(-1).astype(np.int32)


def spread_heads(source_rank, head_index):
    leading_dims = source_rank.shape[:-1]
    reshaped_tensor = source_rank.reshape(leading_dims + (KEY_VALUE_HEADS, HEAD_SIZE))
    taken = jnp.take(reshaped_tensor, head_index, axis=-2)
    return taken


def partial_attention(query_rows, key_matrix, value_matrix, is_live, score_scale):
    scores = (
        jnp.einsum("bkgd,bnkd->bkgn", query_rows, key_matrix, preferred_element_type=jnp.float32)
        * score_scale
    )
    mask = is_live[:, None, None, :]
    scores = jnp.where(mask, scores, -1e30)
    top_score = jnp.max(scores, axis=-1)
    exponent = jnp.where(mask, jnp.exp(scores - top_score[..., None]), 0.0)
    total_mass = jnp.sum(exponent, axis=-1)
    mixture = jnp.einsum(
        "bkgn,bnkd->bkgd",
        exponent.astype(jnp.bfloat16),
        value_matrix,
        preferred_element_type=jnp.float32,
    )
    return (mixture, top_score, total_mass)


def per_device(
    turn_query_rows,
    turn_key_value,
    prefix_page_store,
    prefix_pages,
    holder_table,
    out_weight,
    row_request,
    step_query,
    step_kv,
):
    pool_size = lax.axis_size("pool")
    tensor_split_count = lax.axis_size("tp")
    pool_rank = lax.axis_index("pool")
    tp_rank = lax.axis_index("tp")
    group_width = QUERY_HEADS // KEY_VALUE_HEADS
    heads_dev = QUERY_HEADS // tensor_split_count
    kv_dev = max(1, heads_dev // group_width)
    per_kv = heads_dev // kv_dev
    head_width = kv_dev * HEAD_SIZE
    pages_each_holder = PREFIX_PAGE_CAP // pool_size
    slice_length = PAGE_POSITIONS // tensor_split_count
    score_scale = 1.0 / math.sqrt(HEAD_SIZE)
    head_index = jnp.asarray(head_columns(tensor_split_count, heads_dev, group_width, kv_dev))
    holder_pages_store = prefix_page_store.reshape(
        pool_size, pages_each_holder, 2, slice_length, KEY_VALUE_HEADS * HEAD_SIZE
    )
    spread = spread_heads(holder_pages_store, head_index)
    fetched = lax.all_to_all(
        lax.all_to_all(spread, "pool", split_axis=0, concat_axis=0, tiled=True),
        "tp",
        split_axis=4,
        concat_axis=3,
        tiled=True,
    )
    fetched = fetched.reshape(pool_size * pages_each_holder, 2, PAGE_POSITIONS, head_width)
    holders = lax.dynamic_index_in_dim(holder_table, pool_rank, 0, keepdims=False)
    page_ids = jnp.arange(PREFIX_PAGE_CAP, dtype=jnp.int32)
    prefix = jnp.take(fetched, holders * pages_each_holder + page_ids // pool_size, axis=0)
    local_turn = turn_key_value.reshape(2, turn_key_value.shape[2], KEY_VALUE_HEADS * HEAD_SIZE)
    turn_heads = lax.all_to_all(
        spread_heads(local_turn, head_index), "tp", split_axis=2, concat_axis=1, tiled=True
    )
    turn_pages = jnp.transpose(
        turn_heads.reshape(2, TURN_TOKENS // PAGE_POSITIONS, PAGE_POSITIONS, head_width),
        (1, 0, 2, 3),
    )
    every_page = jnp.concatenate([prefix, turn_pages], axis=0)
    total_pages = every_page.shape[0]
    key_total = total_pages * PAGE_POSITIONS
    my_pages = lax.dynamic_index_in_dim(prefix_pages, pool_rank, 0, keepdims=False)
    position = jnp.arange(key_total, dtype=jnp.int32)
    token_index = jnp.arange(TURN_TOKENS, dtype=jnp.int32)
    is_live = jnp.where(
        position[None, :] < PREFIX_PAGE_CAP * PAGE_POSITIONS,
        position[None, :] // PAGE_POSITIONS < my_pages,
        position[None, :] - PREFIX_PAGE_CAP * PAGE_POSITIONS <= token_index[:, None],
    )
    key_matrix = every_page[:, 0].reshape(key_total, head_width)
    value_matrix = every_page[:, 1].reshape(key_total, head_width)

    def one_head(head):
        query_rows = lax.dynamic_slice_in_dim(turn_query_rows, head * HEAD_SIZE, HEAD_SIZE, 1)
        scores = (
            jnp.einsum("qd,kd->qk", query_rows, key_matrix, preferred_element_type=jnp.float32)
            * score_scale
        )
        scores = jnp.where(is_live, scores, -jnp.inf)
        top_score = jnp.max(scores, axis=1, keepdims=True)
        exponent = jnp.exp(scores - top_score)
        weights = (exponent / jnp.sum(exponent, axis=1, keepdims=True)).astype(jnp.bfloat16)
        return jnp.dot(weights, value_matrix, preferred_element_type=jnp.float32).astype(
            jnp.bfloat16
        )

    heads_out = lax.map(one_head, jnp.arange(heads_dev, dtype=jnp.int32))
    attention = jnp.transpose(heads_out, (1, 0, 2)).reshape(TURN_TOKENS, heads_dev * HEAD_SIZE)
    weight_full = lax.all_gather(out_weight, "pool", axis=1, tiled=True)
    prefill_out = lax.psum_scatter(
        jnp.dot(attention, weight_full, preferred_element_type=jnp.float32).astype(jnp.bfloat16),
        "tp",
        scatter_dimension=0,
        tiled=True,
    )
    slot_count = (total_pages + pool_size - 1) // pool_size
    target_rank = jnp.arange(pool_size, dtype=jnp.int32)[:, None]
    slot_index = jnp.arange(slot_count, dtype=jnp.int32)[None, :]
    wanted = slot_index * pool_size + (target_rank - pool_rank) % pool_size
    outgoing = jnp.take(every_page, jnp.minimum(wanted, total_pages - 1).reshape(-1), axis=0)
    outgoing = outgoing.reshape(pool_size, slot_count, 2, PAGE_POSITIONS, head_width)
    held_pages = lax.all_to_all(outgoing, "pool", split_axis=0, concat_axis=0, tiled=True)
    held_index = slot_index * pool_size + (pool_rank - target_rank) % pool_size
    slot_live = (held_index < total_pages) & (
        (held_index < prefix_pages[:, None]) | (held_index >= PREFIX_PAGE_CAP)
    )
    kv_start = tp_rank * heads_dev // group_width
    output_columns = KEY_VALUE_HEADS * HEAD_SIZE // tensor_split_count
    column_offset = tp_rank * output_columns - kv_start * HEAD_SIZE
    owned_columns = lax.dynamic_slice_in_dim(held_pages, column_offset, output_columns, 4)
    slot_exists = (held_index < total_pages)[:, :, None, None, None]
    decode_cache = jnp.where(slot_exists, owned_columns, jnp.zeros_like(owned_columns))[None]
    local_rows = step_query.shape[1]
    row_total = pool_size * local_rows
    row_block = min(64, row_total)
    block_count = row_total // row_block
    fresh_key_value = lax.dynamic_slice_in_dim(step_kv, kv_start * HEAD_SIZE, head_width, 3)
    requests = row_request.reshape(block_count, row_block)

    def one_block(inputs):
        chosen, query_rows = inputs
        gathered = jnp.take(held_pages, chosen, axis=0)
        block_keys = gathered[:, :, 0].reshape(
            row_block, slot_count * PAGE_POSITIONS, kv_dev, HEAD_SIZE
        )
        block_values = gathered[:, :, 1].reshape(
            row_block, slot_count * PAGE_POSITIONS, kv_dev, HEAD_SIZE
        )
        block_live = jnp.repeat(jnp.take(slot_live, chosen, axis=0), PAGE_POSITIONS, axis=1)
        mixture, top_score, total_mass = partial_attention(
            query_rows.reshape(row_block, kv_dev, per_kv, HEAD_SIZE),
            block_keys,
            block_values,
            block_live,
            score_scale,
        )
        return (
            mixture.reshape(row_block, heads_dev, HEAD_SIZE),
            top_score.reshape(row_block, heads_dev),
            total_mass.reshape(row_block, heads_dev),
        )

    results = []
    for step_index in range(DECODE_STEPS):
        own_queries = step_query[step_index]
        every_query = lax.all_gather(own_queries, "pool", axis=0, tiled=True)
        block_out = lax.map(
            one_block,
            (requests, every_query.reshape(block_count, row_block, heads_dev * HEAD_SIZE)),
        )
        mixture = block_out[0].reshape(row_total, heads_dev, HEAD_SIZE)
        top_score = block_out[1].reshape(row_total, heads_dev)
        total_mass = block_out[2].reshape(row_total, heads_dev)
        own_keys = jnp.transpose(fresh_key_value[: step_index + 1, :, 0], (1, 0, 2)).reshape(
            local_rows, step_index + 1, kv_dev, HEAD_SIZE
        )
        own_values = jnp.transpose(fresh_key_value[: step_index + 1, :, 1], (1, 0, 2)).reshape(
            local_rows, step_index + 1, kv_dev, HEAD_SIZE
        )
        own_live = jnp.ones((local_rows, step_index + 1), dtype=bool)
        own_mixture, own_top, own_total = partial_attention(
            own_queries.reshape(local_rows, kv_dev, per_kv, HEAD_SIZE),
            own_keys,
            own_values,
            own_live,
            score_scale,
        )
        own_mixture = own_mixture.reshape(local_rows, heads_dev, HEAD_SIZE)
        own_top = own_top.reshape(local_rows, heads_dev)
        own_total = own_total.reshape(local_rows, heads_dev)
        parts_mixture, parts_top, parts_total = (
            lax.all_to_all(
                mixture.reshape(pool_size, local_rows, heads_dev, HEAD_SIZE).astype(jnp.bfloat16),
                "pool",
                split_axis=0,
                concat_axis=0,
                tiled=True,
            ).astype(jnp.float32),
            lax.all_to_all(
                top_score.reshape(pool_size, local_rows, heads_dev).astype(jnp.bfloat16),
                "pool",
                split_axis=0,
                concat_axis=0,
                tiled=True,
            ).astype(jnp.float32),
            lax.all_to_all(
                total_mass.reshape(pool_size, local_rows, heads_dev).astype(jnp.bfloat16),
                "pool",
                split_axis=0,
                concat_axis=0,
                tiled=True,
            ).astype(jnp.float32),
        )
        peak_score = jnp.maximum(jnp.max(parts_top, axis=0), own_top)
        factor = jnp.exp(parts_top - peak_score)
        numerator = jnp.sum(parts_mixture * factor[..., None], axis=0)
        denominator = jnp.sum(parts_total * factor, axis=0)
        own_factor = jnp.exp(own_top - peak_score)
        numerator = numerator + own_mixture * own_factor[..., None]
        denominator = denominator + own_total * own_factor
        result = (numerator / denominator[..., None]).astype(jnp.bfloat16)
        results.append(result.reshape(local_rows, heads_dev * HEAD_SIZE))
    decode_out = jnp.stack(results, axis=0)
    return (prefill_out, decode_out, decode_cache)


def solution(mesh):
    placed = (
        P("pool", "tp"),
        P("pool", None, "tp", None),
        P("pool", None, "tp", None),
        P(),
        P(),
        P("tp", "pool"),
        P(),
        P(None, "pool", "tp"),
        P(None, "pool", None, None),
    )
    return jax.shard_map(
        per_device,
        mesh=mesh,
        in_specs=placed,
        out_specs=(
            P(("pool", "tp"), None),
            P(None, "pool", "tp"),
            P("pool", None, None, None, None, "tp"),
        ),
        check_vma=False,
    )
```

profile of v0, /device:TPU:7, one launch (start us, length us, event | category | flops | bytes accessed | tf_op | source)
XLA Modules:
  0.0 518.5 jit_solution(3263297655749832826)
XLA Ops:
  9.6 1.5 copy.131
  11.1 16.4 %all-to-all-start = ((bf16[32,1,2,4,16,128]{5,3,2,4,1,0:T(4,128)(2,1)}), bf16[32,1,2,4,16,128]{5,3,2,4,1,0:T(4,128)(2,1)S(1)}, u32[]{:S(2)}, u32[]{:S(2)}) async-start(bf16[32,1,2,4,16,128]{5,3,2,4,1,0:T(4,128)(2,1)} %copy.131), calls=%async_computation | async-start | bytes 2097152 | tf_op jit(solution)/shard_map/all_to_all | solution.py:79
  29.6 29.1 %all-to-all-done = bf16[32,1,2,4,16,128]{5,3,2,4,1,0:T(4,128)(2,1)S(1)} async-done(((bf16[32,1,2,4,16,128]{5,3,2,4,1,0:T(4,128)(2,1)}), bf16[32,1,2,4,16,128]{5,3,2,4,1,0:T(4,128)(2,1)S(1)}, u32[]{:S(2)}, u32[]{:S(2)}) %all-to-all-start) | async-done | bytes 1048608 | tf_op jit(solution)/shard_map/all_to_all | solution.py:79
  58.7 7.0 %all-to-all-start.2 = ((bf16[2,16,16,128]{3,1,0,2:T(8,128)(2,1)}), bf16[2,16,16,128]{3,1,0,2:T(8,128)(2,1)S(1)}, u32[]{:S(2)}, u32[]{:S(2)}) async-start(bf16[2,16,16,128]{3,1,0,2:T(8,128)(2,1)} %bitcast.8), calls=%async_computation.2 | async-start | bytes 262144 | tf_op jit(solution)/shard_map/all_to_all | solution.py:90
  65.8 2.2 copy.132
  67.9 3.3 all-to-all-done.2
  71.2 5.3 %all-to-all-start.1 = ((bf16[32,1,2,4,16,128]{5,0,3,2,1,4:T(8,128)(2,1)}), bf16[32,1,2,4,16,128]{5,0,3,2,1,4:T(8,128)(2,1)S(1)}, u32[]{:S(2)}, u32[]{:S(2)}) async-start(bf16[32,1,2,4,16,128]{5,0,3,2,1,4:T(8,128)(2,1)} %copy.132), calls=%async_computation.1 | async-start | bytes 2097152 | tf_op jit(solution)/shard_map/all_to_all | solution.py:78
  88.5 63.8 %all-gather.1 = bf16[1,256,512]{2,1,0:T(8,128)(2,1)S(1)} all-gather(bf16[1,8,512]{2,1,0:T(8,128)(2,1)S(1)} %get-tuple-element.349), channel_id=3, replica_groups=mesh['pool'=32,'tp'=16] {'pool'}, dimensions={1}, use_global_device_ids=true | all-gather | bytes 270336 | tf_op jit(solution)/shard_map/all_gather | solution.py:184
  152.3 50.3 %all-gather = bf16[1,256,512]{2,1,0:T(8,128)(2,1)} all-gather(bf16[1,8,512]{2,1,0:T(8,128)(2,1)S(1)} %get-tuple-element.350), channel_id=2, replica_groups=mesh['pool'=32,'tp'=16] {'pool'}, dimensions={1}, use_global_device_ids=true | all-gather | bytes 270336 | tf_op jit(solution)/shard_map/all_gather | solution.py:184
  206.4 2.3 broadcast_select_fusion.4
  208.7 7.4 %all-to-all-start.3 = ((bf16[32,2,2,64,128]{4,3,2,1,0:T(8,128)(2,1)}), bf16[32,2,2,64,128]{4,3,2,1,0:T(8,128)(2,1)S(1)}, u32[]{:S(2)}, u32[]{:S(2)}) async-start(bf16[32,2,2,64,128]{4,3,2,1,0:T(8,128)(2,1)} %broadcast_select_fusion.4), calls=%async_computation.4 | async-start | bytes 4194304 | tf_op jit(solution)/shard_map/all_to_all | solution.py:140
  216.2 17.9 %while.41 = (s32[]{:T(128)}, bf16[4,256,128]{1,2,0:T(8,128)(2,1)S(1)}, s32[4]{0:T(128)S(1)}, bf16[256,512]{1,0:T(8,128)(2,1)}, bf16[2304,128]{1,0:T(8,128)(2,1)}...) while((s32[]{:T(128)}, ...), condition=%wide.region_3.4_spmd.clone, body=%wide.region_0.3_spmd.clone.sunk | while | flops 307920384 | bytes 8669895 | solution.py:125
  217.4 2.0 fusion.101
  221.9 2.0 fusion.101
  226.4 2.0 fusion.101
  230.9 2.0 fusion.101
  234.1 37.6 %all-to-all-done.3 = bf16[32,2,2,64,128]{4,3,2,1,0:T(8,128)(2,1)S(1)} async-done(((bf16[32,2,2,64,128]{4,3,2,1,0:T(8,128)(2,1)}), bf16[32,2,2,64,128]{4,3,2,1,0:T(8,128)(2,1)S(1)}, u32[]{:S(2)}, u32[]{:S(2)}) %all-to-all-start.3) | async-done | bytes 2097184 | tf_op jit(solution)/shard_map/all_to_all | solution.py:140
  272.5 61.5 %while.42 = (s32[]{:T(128)}, bf16[4,64,4,128]{3,2,1,0:T(4,128)(2,1)}, bf16[4,64,4]{2,1,0:T(8,128)(2,1)S(1)}, bf16[4,64,4]{2,1,0:T(8,128)(2,1)S(1)}, s32[4,64]{1,...) while((s32[]{:T(128)}, ...), condition=%wide.region_8.11_spmd.clone, body=%wide.region_5.10_spmd.clone.sunk | while | flops 19170688 | bytes 38758828 | solution.py:185
  272.5 3.1 gather_fusion
  275.6 2.6 broadcast_select_fusion.10
  278.3 3.0 fusion.108
  283.2 3.0 fusion.109
  287.9 3.1 gather_fusion
  291.0 2.6 broadcast_select_fusion.10
  293.6 3.0 fusion.108
  298.6 3.0 fusion.109
  303.3 3.1 gather_fusion
  306.4 2.6 broadcast_select_fusion.10
  309.0 3.0 fusion.108
  314.0 3.0 fusion.109
  318.6 3.1 gather_fusion
  321.7 2.6 broadcast_select_fusion.10
  324.4 3.0 fusion.108
  329.3 3.0 fusion.109
  334.8 17.5 %all-to-all-start.5 = ((bf16[32,8,4]{1,2,0:T(4,128)(2,1)}), bf16[32,8,4]{1,2,0:T(4,128)(2,1)S(1)}, u32[]{:S(2)}, u32[]{:S(2)}) async-start(bf16[32,8,4]{1,2,0:T(4,128)(2,1)} %copy.142), calls=%async_computation.6 | async-start | bytes 65536 | tf_op jit(solution)/shard_map/all_to_all | solution.py:217
  352.5 4.8 convolution_convert_fusion
  358.1 57.8 %while.43 = (s32[]{:T(128)}, bf16[4,64,4,128]{3,2,1,0:T(4,128)(2,1)}, bf16[4,64,4]{2,1,0:T(8,128)(2,1)S(1)}, bf16[4,64,4]{2,1,0:T(8,128)(2,1)S(1)}, s32[4,64]{1,...) while((s32[]{:T(128)}, ...), condition=%wide.region_15.18_spmd.clone, body=%wide.region_12.17_spmd.clone.sunk | while | flops 19170688 | bytes 38758828 | solution.py:185
  358.1 3.0 gather_fusion.2
  361.2 2.6 broadcast_select_fusion.12
  363.8 3.0 fusion.116
  367.9 3.0 fusion.117
  372.6 3.0 gather_fusion.2
  375.6 2.6 broadcast_select_fusion.12
  378.3 3.0 fusion.116
  382.4 3.0 fusion.117
  387.1 3.0 gather_fusion.2
  390.1 2.6 broadcast_select_fusion.12
  392.7 3.0 fusion.116
  396.9 3.0 fusion.117
  401.5 3.0 gather_fusion.2
  404.6 2.6 broadcast_select_fusion.12
  407.2 3.0 fusion.116
  411.3 3.0 fusion.117
  416.8 12.2 %all-to-all-start.6 = ((bf16[32,8,4]{1,2,0:T(4,128)(2,1)}), bf16[32,8,4]{1,2,0:T(4,128)(2,1)S(1)}, u32[]{:S(2)}, u32[]{:S(2)}) async-start(bf16[32,8,4]{1,2,0:T(4,128)(2,1)} %copy.149), calls=%async_computation.7 | async-start | bytes 65536 | tf_op jit(solution)/shard_map/all_to_all | solution.py:224
  429.1 2.4 select_bitcast_fusion
  433.2 7.8 %all-to-all-done.6 = bf16[32,8,4]{1,2,0:T(4,128)(2,1)S(1)} async-done(((bf16[32,8,4]{1,2,0:T(4,128)(2,1)}), bf16[32,8,4]{1,2,0:T(4,128)(2,1)S(1)}, u32[]{:S(2)}, u32[]{:S(2)}) %all-to-all-start.6) | async-done | bytes 2080 | tf_op jit(solution)/shard_map/all_to_all | solution.py:224
  441.0 4.4 all-to-all-start.8
  445.6 11.8 %all-to-all-done.8 = bf16[32,8,4]{1,2,0:T(4,128)(2,1)S(1)} async-done(((bf16[32,8,4]{1,2,0:T(4,128)(2,1)}), bf16[32,8,4]{1,2,0:T(4,128)(2,1)S(1)}, u32[]{:S(2)}, u32[]{:S(2)}) %all-to-all-start.8) | async-done | bytes 2080 | tf_op jit(solution)/shard_map/all_to_all | solution.py:217
  457.5 3.9 all-to-all-start.9
  461.6 11.9 %all-to-all-done.9 = bf16[32,8,4]{1,2,0:T(4,128)(2,1)S(1)} async-done(((bf16[32,8,4]{1,2,0:T(4,128)(2,1)}), bf16[32,8,4]{1,2,0:T(4,128)(2,1)S(1)}, u32[]{:S(2)}, u32[]{:S(2)}) %all-to-all-start.9) | async-done | bytes 2080 | tf_op jit(solution)/shard_map/all_to_all | solution.py:224
  473.5 3.9 all-to-all-start.7
  477.8 13.3 %all-to-all-done.7 = bf16[32,8,4,128]{3,2,1,0:T(4,128)(2,1)S(1)} async-done(((bf16[32,8,4,128]{3,2,1,0:T(4,128)(2,1)}), bf16[32,8,4,128]{3,2,1,0:T(4,128)(2,1)S(1)}, u32[]{:S(2)}, u32[]{:S(2)}) %all-to-all-start.7) | async-done | bytes 262176 | tf_op jit(solution)/shard_map/all_to_all | solution.py:210
  491.1 5.9 %all-to-all-start.4 = ((bf16[32,8,4,128]{3,2,1,0:T(4,128)(2,1)}), bf16[32,8,4,128]{3,2,1,0:T(4,128)(2,1)S(1)}, u32[]{:S(2)}, u32[]{:S(2)}) async-start(bf16[32,8,4,128]{3,2,1,0:T(4,128)(2,1)} %bitcast.21), calls=%async_computation.5 | async-start | bytes 524288 | tf_op jit(solution)/shard_map/all_to_all | solution.py:210
  498.3 12.3 %all-to-all-done.4 = bf16[32,8,4,128]{3,2,1,0:T(4,128)(2,1)S(1)} async-done(((bf16[32,8,4,128]{3,2,1,0:T(4,128)(2,1)}), bf16[32,8,4,128]{3,2,1,0:T(4,128)(2,1)S(1)}, u32[]{:S(2)}, u32[]{:S(2)}) %all-to-all-start.4) | async-done | bytes 262176 | tf_op jit(solution)/shard_map/all_to_all | solution.py:210
  (286 shorter events, 61.1 us)
Async XLA Ops:
  7.2 1.6 copy-start.21
  9.6 18.7 %copy-start.4 = (bf16[1,2,16,1024]{3,2,1,0:T(8,128)(2,1)S(1)}, bf16[1,2,16,1024]{3,2,1,0:T(8,128)(2,1)}, u32[]{:S(2)}) copy-start(bf16[1,2,16,1024]{3,2,1,0:T(8,128)(2,1)} %param.21) | copy-start | bytes 196612
  9.6 56.2 %copy-start.10 = (bf16[2,8,512]{2,1,0:T(8,128)(2,1)S(1)}, bf16[2,8,512]{2,1,0:T(8,128)(2,1)}, u32[]{:S(2)}) copy-start(bf16[2,8,512]{2,1,0:T(8,128)(2,1)} %param.27) | copy-start | bytes 49156
  11.1 47.6 %all-to-all-start = ((bf16[32,1,2,4,16,128]{5,3,2,4,1,0:T(4,128)(2,1)}), bf16[32,1,2,4,16,128]{5,3,2,4,1,0:T(4,128)(2,1)S(1)}, u32[]{:S(2)}, u32[]{:S(2)}) async-start(bf16[32,1,2,4,16,128]{5,3,2,4,1,0:T(4,128)(2,1)} %copy.131), calls=%async_computation | async-start | bytes 2097152 | tf_op jit(solution)/shard_map/all_to_all | solution.py:79
  27.5 324.9 %all-gather.4.cloned.1.call-start = ((), (), s32[]{:S(2)}) async-start(), calls=%async_computation.11 | async-start | bytes 4325376 | tf_op jit(solution)/shard_map/all_gather | solution.py:127
  58.7 12.5 %all-to-all-start.2 = ((bf16[2,16,16,128]{3,1,0,2:T(8,128)(2,1)}), bf16[2,16,16,128]{3,1,0,2:T(8,128)(2,1)S(1)}, u32[]{:S(2)}, u32[]{:S(2)}) async-start(bf16[2,16,16,128]{3,1,0,2:T(8,128)(2,1)} %bitcast.8), calls=%async_computation.2 | async-start | bytes 262144 | tf_op jit(solution)/shard_map/all_to_all | solution.py:90
  65.7 10.9 %copy-start.20 = (s32[256]{0:T(256)S(1)}, s32[256]{0:T(256)}, u32[]{:S(2)}) copy-start(s32[256]{0:T(256)} %param.26) | copy-start | bytes 3076
  65.7 16.9 %copy-start.5 = (s32[32]{0:T(128)S(1)}, s32[32]{0:T(128)}, u32[]{:S(2)}) copy-start(s32[32]{0:T(128)} %param.23) | copy-start | bytes 388
  71.2 131.4 %all-to-all-start.1 = ((bf16[32,1,2,4,16,128]{5,0,3,2,1,4:T(8,128)(2,1)}), bf16[32,1,2,4,16,128]{5,0,3,2,1,4:T(8,128)(2,1)S(1)}, u32[]{:S(2)}, u32[]{:S(2)}) async-start(bf16[32,1,2,4,16,128]{5,0,3,2,1,4:T(8,128)(2,1)} %copy.132), calls=%async_computation.1 | async-start | bytes 2097152 | tf_op jit(solution)/shard_map/all_to_all | solution.py:78
  79.1 123.4 %copy-start.11 = (f32[8,4]{1,0:T(8,128)}, f32[8,4]{1,0:T(8,128)S(1)}, u32[]{:S(2)}) copy-start(f32[8,4]{1,0:T(8,128)S(1)} %get-tuple-element.360) | copy-start | bytes 388
  79.2 123.4 %copy-start.14 = (f32[8,4,2]{1,2,0:T(2,128)}, f32[8,4,2]{1,2,0:T(2,128)S(1)}, u32[]{:S(2)}) copy-start(f32[8,4,2]{1,2,0:T(2,128)S(1)} %get-tuple-element.361) | copy-start | bytes 772
  208.6 7.5 %copy-start.2 = (bf16[36,1,64,128]{3,2,1,0:T(8,128)(2,1)S(1)}, bf16[36,1,64,128]{3,2,1,0:T(8,128)(2,1)}, u32[]{:S(2)}) copy-start(bf16[36,1,64,128]{3,2,1,0:T(8,128)(2,1)} %get-tuple-element.344) | copy-start | bytes 1769476
  208.7 7.5 %copy-start.3 = (bf16[4,256,128]{1,2,0:T(8,128)(2,1)S(1)}, bf16[4,256,128]{1,2,0:T(8,128)(2,1)}, u32[]{:S(2)}) copy-start(bf16[4,256,128]{1,2,0:T(8,128)(2,1)} %custom-call.16) | copy-start | bytes 786436
  208.7 7.5 %copy-start.13 = (s32[2304]{0:T(1024)S(1)}, s32[2304]{0:T(1024)}, u32[]{:S(2)}) copy-start(s32[2304]{0:T(1024)} %iota_add_fusion) | copy-start | bytes 27652
  208.7 7.5 %copy-start.18 = (pred[2304]{0:T(1024)(128)(4,1)S(1)}, pred[2304]{0:T(1024)(128)(4,1)}, u32[]{:S(2)}) copy-start(pred[2304]{0:T(1024)(128)(4,1)} %get-tuple-element.576) | copy-start | bytes 6916
  208.7 7.5 %copy-start.19 = (pred[2304]{0:T(1024)(128)(4,1)S(1)}, pred[2304]{0:T(1024)(128)(4,1)}, u32[]{:S(2)}) copy-start(pred[2304]{0:T(1024)(128)(4,1)} %get-tuple-element.577) | copy-start | bytes 6916
  208.7 63.0 %all-to-all-start.3 = ((bf16[32,2,2,64,128]{4,3,2,1,0:T(8,128)(2,1)}), bf16[32,2,2,64,128]{4,3,2,1,0:T(8,128)(2,1)S(1)}, u32[]{:S(2)}, u32[]{:S(2)}) async-start(bf16[32,2,2,64,128]{4,3,2,1,0:T(8,128)(2,1)} %broadcast_select_fusion.4), calls=%async_computation.4 | async-start | bytes 4194304 | tf_op jit(solution)/shard_map/all_to_all | solution.py:140
  283.2 3.0 copy-start
  298.6 3.0 copy-start
  314.0 3.0 copy-start
  329.3 3.0 copy-start
  334.8 82.0 %all-to-all-start.5 = ((bf16[32,8,4]{1,2,0:T(4,128)(2,1)}), bf16[32,8,4]{1,2,0:T(4,128)(2,1)S(1)}, u32[]{:S(2)}, u32[]{:S(2)}) async-start(bf16[32,8,4]{1,2,0:T(4,128)(2,1)} %copy.142), calls=%async_computation.6 | async-start | bytes 65536 | tf_op jit(solution)/shard_map/all_to_all | solution.py:217
  352.4 159.3 %reduce-scatter.2.cloned.1.call-start = ((), (), s32[]{:S(2)}) async-start(), calls=%async_computation.12 | async-start | bytes 2228224 | tf_op jit(solution)/shard_map/reduce_scatter | solution.py:128
  358.1 71.0 %copy-start.8 = (pred[32,2]{1,0:T(8,128)(4,1)S(1)}, pred[32,2]{1,0:T(8,128)(4,1)}, u32[]{:S(2)}) copy-start(pred[32,2]{1,0:T(8,128)(4,1)} %copy.167) | copy-start | bytes 196
  367.9 3.0 copy-start.1
  382.4 3.0 copy-start.1
  396.8 3.0 copy-start.1
  411.3 3.0 copy-start.1
  416.8 24.2 %all-to-all-start.6 = ((bf16[32,8,4]{1,2,0:T(4,128)(2,1)}), bf16[32,8,4]{1,2,0:T(4,128)(2,1)S(1)}, u32[]{:S(2)}, u32[]{:S(2)}) async-start(bf16[32,8,4]{1,2,0:T(4,128)(2,1)} %copy.149), calls=%async_computation.7 | async-start | bytes 65536 | tf_op jit(solution)/shard_map/all_to_all | solution.py:224
  429.1 16.4 %copy-start.7 = (f32[8,1,4]{0,2,1:T(4,128)S(1)}, f32[8,1,4]{0,2,1:T(4,128)}, u32[]{:S(2)}) copy-start(f32[8,1,4]{0,2,1:T(4,128)} %copy.170) | copy-start | bytes 388
  429.1 48.3 %copy-start.6 = (f32[8,4]{0,1:T(4,128)S(1)}, f32[8,4]{0,1:T(4,128)}, u32[]{:S(2)}) copy-start(f32[8,4]{0,1:T(4,128)} %copy.157) | copy-start | bytes 388
  429.1 67.9 %copy-start.16 = (f32[8,4]{0,1:T(4,128)S(1)}, f32[8,4]{0,1:T(4,128)}, u32[]{:S(2)}) copy-start(f32[8,4]{0,1:T(4,128)} %copy.165) | copy-start | bytes 388
  431.4 66.6 %copy-start.12 = (f32[8,4]{1,0:T(8,128)S(1)}, f32[8,4]{1,0:T(8,128)}, u32[]{:S(2)}) copy-start(f32[8,4]{1,0:T(8,128)} %copy-done.11) | copy-start | bytes 388
  431.5 66.6 %copy-start.15 = (f32[8,4,2]{1,2,0:T(2,128)S(1)}, f32[8,4,2]{1,2,0:T(2,128)}, u32[]{:S(2)}) copy-start(f32[8,4,2]{1,2,0:T(2,128)} %copy-done.14) | copy-start | bytes 772
  431.5 66.6 %copy-start.17 = (bf16[2,8,1,128]{3,2,1,0:T(2,128)(2,1)S(1)}, bf16[2,8,1,128]{3,2,1,0:T(2,128)(2,1)}, u32[]{:S(2)}) copy-start(bf16[2,8,1,128]{3,2,1,0:T(2,128)(2,1)} %get-tuple-element.346) | copy-start | bytes 12292
  431.5 79.5 %copy-start.9 = (f32[1,8,1,128]{3,0,1,2:T(1,128)S(1)}, f32[1,8,1,128]{3,0,1,2:T(1,128)}, u32[]{:S(2)}) copy-start(f32[1,8,1,128]{3,0,1,2:T(1,128)} %fusion.50) | copy-start | bytes 12292
  441.0 16.4 %all-to-all-start.8 = ((bf16[32,8,4]{1,2,0:T(4,128)(2,1)}), bf16[32,8,4]{1,2,0:T(4,128)(2,1)S(1)}, u32[]{:S(2)}, u32[]{:S(2)}) async-start(bf16[32,8,4]{1,2,0:T(4,128)(2,1)} %copy.154), calls=%async_computation.9 | async-start | bytes 65536 | tf_op jit(solution)/shard_map/all_to_all | solution.py:217
  457.5 16.0 %all-to-all-start.9 = ((bf16[32,8,4]{1,2,0:T(4,128)(2,1)}), bf16[32,8,4]{1,2,0:T(4,128)(2,1)S(1)}, u32[]{:S(2)}, u32[]{:S(2)}) async-start(bf16[32,8,4]{1,2,0:T(4,128)(2,1)} %copy.162), calls=%async_computation.10 | async-start | bytes 65536 | tf_op jit(solution)/shard_map/all_to_all | solution.py:224
  473.5 17.6 %all-to-all-start.7 = ((bf16[32,8,4,128]{3,2,1,0:T(4,128)(2,1)}), bf16[32,8,4,128]{3,2,1,0:T(4,128)(2,1)S(1)}, u32[]{:S(2)}, u32[]{:S(2)}) async-start(bf16[32,8,4,128]{3,2,1,0:T(4,128)(2,1)} %bitcast.29), calls=%async_computation.8 | async-start | bytes 524288 | tf_op jit(solution)/shard_map/all_to_all | solution.py:210
  491.1 19.5 %all-to-all-start.4 = ((bf16[32,8,4,128]{3,2,1,0:T(4,128)(2,1)}), bf16[32,8,4,128]{3,2,1,0:T(4,128)(2,1)S(1)}, u32[]{:S(2)}, u32[]{:S(2)}) async-start(bf16[32,8,4,128]{3,2,1,0:T(4,128)(2,1)} %bitcast.21), calls=%async_computation.5 | async-start | bytes 524288 | tf_op jit(solution)/shard_map/all_to_all | solution.py:210
Sparse Core Ops, SparseCore 0:
  31.5 116.3 all-gather.3
  357.4 77.0 reduce-scatter.1
where the time goes:
time: 520 us; the launch traced here: 519 us
  waiting for transfers between devices  128 us (25%)
  blocking collectives  114 us (22%)
  local copies, waits for them, and re-layouts  84 us (16%)
  starting transfers between devices  83.9 us (16%)
  matrix products  51.2 us (10%)
  other arithmetic  39.5 us (8%)
  between operations  14.6 us (3%)
    all_gather x2, blocking collectives, per_device(): every_query = lax.all_gather(own_queries, 'pool', axis=0, tiled=True)  114 us
    all_to_all x1, waiting for transfers between devices, per_device(): lax.all_to_all(outgoing, 'pool', split_axis=0, concat_axis=0, tiled=True)  37.6 us
    all_to_all x1, waiting for transfers between devices, per_device(): lax.all_to_all(spread, 'pool', split_axis=0, concat_axis=0, tiled=True)  29.1 us
    all_to_all x2, waiting for transfers between devices, per_device(): lax.all_to_all(mixture.reshape(pool_size, local_rows, heads_dev, HEAD_SIZ...  25.6 us
    dot_general x10, matrix products, partial_attention(): jnp.einsum('bkgd,bnkd->bkgn', query_rows, key_matrix, preferred_element_t...  25 us
    gather x8, local copies, waits for them, and re-layouts, one_block(): gathered = jnp.take(held_pages, chosen, axis=0)  24.4 us
    slice x8, local copies, waits for them, and re-layouts, one_block(): gathered[:, :, 0]  23.9 us
    all_to_all x2, starting transfers between devices, per_device(): lax.all_to_all(top_score.reshape(pool_size, local_rows, heads_dev).astype...  21.9 us
  transfers between devices with their start and end apart: 12, of which 8 were waited for; matrix products, arithmetic and copies ran while one was open for 33% of the time, Pallas kernels for 0%

commit v1 on v0

v1 whole, which is shorter than its diff:
```python
import functools
import math

import jax
import jax.numpy as jnp
import numpy as np
from jax import lax
from jax.experimental import pallas as pl
from jax.experimental.pallas import tpu as pltpu
from jax.sharding import PartitionSpec as P

QUERY_HEADS = 64
KEY_VALUE_HEADS = 8
HEAD_SIZE = 128
PAGE_POSITIONS = 64
PREFIX_PAGE_CAP = 32
TURN_TOKENS = 256
DECODE_STEPS = 2
POOL = 32
TP = 16
HEADS_DEV = QUERY_HEADS // TP
SCORE_SCALE = 1.0 / math.sqrt(HEAD_SIZE)
EXP2_SCALE = SCORE_SCALE * math.log2(math.e)
DEAD = 10000.0
WEIGHT_ROWS = 512
QUERY_ROWS = 64
FRESH_ROWS = 32
BLOCK_ROWS = WEIGHT_ROWS + QUERY_ROWS + FRESH_ROWS
SLOT_ROWS = 144
KEYS = TP * SLOT_ROWS
DECODE_BLOCK = 16
VMEM_LIMIT = 56 * 1024 * 1024

MESH = pl.DeviceIdType.MESH
NT = (((1,), (1,)), ((), ()))
TN = (((0,), (0,)), ((), ()))


def remote(src, dst, send_sem, recv_sem, **axes):
    return pltpu.make_async_remote_copy(
        src_ref=src,
        dst_ref=dst,
        send_sem=send_sem,
        recv_sem=recv_sem,
        device_id=axes,
        device_id_type=MESH,
    )


def half_columns(keys, values, parity):
    low = lax.broadcasted_iota(jnp.int32, keys.shape, 1) < 64
    even = jnp.where(low, keys, pltpu.roll(values, 64, 1))
    odd = jnp.where(low, pltpu.roll(keys, 64, 1), values)
    return jnp.where(parity == 0, even, odd).astype(jnp.bfloat16)


def fetch_kernel(
    store,
    turn,
    block,
    query,
    limit,
    in_code,
    row_code,
    mixer,
    attention,
    cache_kv,
    gathered,
    pages_in,
    turn_in,
    fetched,
    by_head,
    pages_out,
    turn_out,
    page_pick,
    fetch_send,
    fetch_recv,
    head_send,
    head_recv,
    page_send,
    page_recv,
    turn_send,
    turn_recv,
    ring_send,
    ring_recv,
    pair_send,
    pair_recv,
    core_send,
    core_recv,
    own_sem,
):
    me = lax.axis_index("pool")
    rank = lax.axis_index("tp")
    z = me // 4
    y_hi = (me // 2) % 2
    core = me % 2
    other_core = me + 1 - 2 * core
    partner = me + 2 - 4 * y_hi

    barrier = pltpu.get_barrier_semaphore()

    def greet_pool(i, carry):
        pl.semaphore_signal(
            barrier, inc=1, device_id={"pool": (me + i) % POOL}, device_id_type=MESH
        )
        return carry

    def greet_tp(i, carry):
        pl.semaphore_signal(
            barrier, inc=1, device_id={"tp": (rank + i) % TP}, device_id_type=MESH
        )
        return carry

    lax.fori_loop(1, POOL, greet_pool, 0)
    lax.fori_loop(1, TP, greet_tp, 0)
    pl.semaphore_wait(barrier, POOL - 1 + TP - 1)

    def fetch_copy(i):
        to = (me + i) % POOL
        return remote(
            store.at[to], fetched.at[i], fetch_send.at[i], fetch_recv.at[i], pool=to
        )

    def start_fetch(i, carry):
        fetch_copy(i).start()
        return carry

    lax.fori_loop(1, POOL, start_fetch, 0)
    fetched[0] = store[me]

    def place(at_z, at_y):
        return ((at_z + 8) % 8) * 2 + at_y

    def ring_copy(direction, step, at_y, first=False):
        sign = 1 - 2 * direction
        at = place(z - sign * step, at_y)
        to = ((z + sign + 8) % 8) * 4 + y_hi * 2 + core
        slot = gathered.at[core, at]
        return remote(
            block if first else slot,
            slot,
            ring_send.at[direction, step, at_y],
            ring_recv.at[direction, step, at_y],
            pool=to,
        )

    def core_copy(at, first=False):
        slot = gathered.at[core, at]
        return remote(
            block if first else slot, slot, core_send.at[at], core_recv, pool=other_core
        )

    def ring_wait(direction, step, at_y):
        ring_copy(direction, step, at_y).wait_recv()

    def arrived(direction, step, at_y):
        sign = 1 - 2 * direction
        return place(z - sign * (step + 1), at_y)

    own_place = place(z, y_hi)
    pair_place = place(z, 1 - y_hi)
    pair_copy = remote(
        block, gathered.at[core, own_place], pair_send, pair_recv, pool=partner
    )
    pair_copy.start()
    for direction in range(2):
        ring_copy(direction, 0, y_hi, True).start()
    core_copy(own_place, True).start()
    own_copy = pltpu.make_async_copy(block, gathered.at[core, own_place], own_sem)
    own_copy.start()

    mix = mixer[...]

    def regroup(rows, group, kv):
        moved = jnp.dot(mix, rows, preferred_element_type=jnp.float32).astype(jnp.bfloat16)
        by_head[:, kv, pl.ds(group * 16, 16), :] = moved.reshape(KEY_VALUE_HEADS, 16, HEAD_SIZE)

    for kv in range(2):
        regroup(turn[kv], 8, kv)

    def head_copy(i, part):
        to = (rank + i) % TP
        rows = pl.ds(part * 64, 64 + 16 * part)
        return remote(
            by_head.at[to // 2, :, rows],
            cache_kv.at[rank, :, rows],
            head_send.at[part, i],
            head_recv.at[part, rank],
            tp=to,
        )

    def head_arrival(i, part):
        source = (rank + TP - i) % TP
        rows = pl.ds(part * 64, 64 + 16 * part)
        return remote(
            by_head.at[0, :, rows],
            cache_kv.at[source, :, rows],
            head_send.at[part, i],
            head_recv.at[part, source],
            tp=rank,
        )

    def forward_pair():
        pair_copy.wait_recv()
        for direction in range(2):
            ring_copy(direction, 0, 1 - y_hi).start()
        core_copy(pair_place).start()

    def ring_step(step):
        for at_y in range(2):
            for direction in range(2):
                ring_wait(direction, step - 1, at_y)
                if step < 3 or at_y == direction:
                    ring_copy(direction, step, at_y).start()
                core_copy(arrived(direction, step - 1, at_y)).start()

    for part in range(2):
        def one_group(group, carry):
            for k in range(4):
                slot = group * 4 + k

                @pl.when(slot > 0)
                def _():
                    fetch_copy(slot).wait_recv()

            rows = fetched[pl.ds(group * 4, 4)]
            for kv in range(2):
                regroup(rows[:, kv * 32 : kv * 32 + 32].reshape(128, HEAD_SIZE), group, kv)
            return carry

        lax.fori_loop(4 * part, 4 * part + 4, one_group, 0)

        def start_head(i, carry):
            head_copy(i, part).start()
            return carry

        lax.fori_loop(1, TP, start_head, 0)
        if part == 0:
            forward_pair()
    cache_kv[rank] = by_head[rank // 2]
    ring_step(1)

    def wait_heads(i, carry):
        for part in range(2):
            head_arrival(i, part).wait_recv()
        return carry

    lax.fori_loop(1, TP, wait_heads, 0)

    page_pick[...] = jnp.where(row_code[...] == in_code[...], 1.0, 0.0).astype(jnp.bfloat16)
    parity = rank % 2

    def page_group(group, carry):
        picked = []
        for kv in range(2):
            rows = cache_kv[pl.ds(group * 4, 4), kv, :128, :].reshape(512, HEAD_SIZE)
            picked.append(jnp.dot(page_pick[...], rows, preferred_element_type=jnp.float32))
        halves = half_columns(picked[0], picked[1], parity)
        pages_out[:, pl.ds(group * 16, 16), :] = halves.reshape(POOL, 16, HEAD_SIZE)
        rows = [
            cache_kv[pl.ds(group * 4, 4), kv, 128:, :].reshape(64, HEAD_SIZE).astype(jnp.float32)
            for kv in range(2)
        ]
        turn_out[group] = half_columns(rows[0], rows[1], parity)
        return carry

    lax.fori_loop(0, 4, page_group, 0)

    def page_copy(i):
        to = (me + i) % POOL
        return remote(
            pages_out.at[to], pages_in.at[i], page_send.at[i], page_recv.at[i], pool=to
        )

    def turn_copy(i):
        return remote(
            turn_out.at[i],
            turn_in.at[i],
            turn_send.at[i],
            turn_recv.at[i],
            pool=(me + i) % POOL,
        )

    def start_page(i, carry):
        page_copy(i).start()
        return carry

    lax.fori_loop(1, POOL, start_page, 0)
    for i in range(1, 4):
        turn_copy(i).start()
    pages_in[0] = pages_out[me]
    turn_in[0] = turn_out[0]

    def one_head(head):
        columns = slice(head * HEAD_SIZE, (head + 1) * HEAD_SIZE)
        keys = cache_kv[:, 0].reshape(KEYS, HEAD_SIZE)
        values = cache_kv[:, 1].reshape(KEYS, HEAD_SIZE)

        def rows_block(b, carry):
            at = pl.ds(b * 128, 128)
            scores = lax.dot_general(
                query[at, columns], keys, NT, preferred_element_type=jnp.float32
            )
            token = lax.broadcasted_iota(jnp.int32, (128, KEYS), 0) + b * 128
            scores = jnp.where(limit[...] <= token.astype(jnp.float32), scores, -jnp.inf)
            top = jnp.max(scores, axis=1, keepdims=True)
            exponent = jnp.exp2(scores * EXP2_SCALE - top * EXP2_SCALE)
            total = jnp.sum(exponent, axis=1, keepdims=True)
            mixed = jnp.dot(
                exponent.astype(jnp.bfloat16), values, preferred_element_type=jnp.float32
            )
            attention[at, columns] = (mixed / total).astype(jnp.bfloat16)
            return carry

        lax.fori_loop(0, 2, rows_block, 0)

    one_head(0)
    ring_step(2)
    one_head(1)
    ring_step(3)
    one_head(2)
    for direction in range(2):
        ring_wait(direction, 3, direction)
        core_copy(arrived(direction, 3, direction)).start()
    one_head(3)

    def finish_pool(i, carry):
        fetch_copy(i).wait_send()
        page_copy(i).wait()
        return carry

    lax.fori_loop(1, POOL, finish_pool, 0)
    for i in range(1, 4):
        turn_copy(i).wait()

    def finish_tp(i, carry):
        for part in range(2):
            head_copy(i, part).wait_send()
        return carry

    lax.fori_loop(1, TP, finish_tp, 0)
    own_copy.wait()
    pair_copy.wait_send()
    for step in range(4):
        for at_y in range(2):
            for direction in range(2):
                if step < 3 or at_y == direction:
                    ring_copy(direction, step, at_y).wait_send()

    def finish_core(i, carry):
        core_copy(i).wait_send()
        return carry

    lax.fori_loop(0, 16, finish_core, 0)
    everything = gathered.at[1 - core]
    pltpu.make_async_copy(everything, everything, core_recv).wait()


def fetch_call(*operands):
    vmem = pl.BlockSpec(memory_space=pltpu.VMEM)
    dma = pltpu.SemaphoreType.DMA
    return pl.pallas_call(
        fetch_kernel,
        out_shape=(
            jax.ShapeDtypeStruct((TURN_TOKENS, HEADS_DEV * HEAD_SIZE), jnp.bfloat16),
            jax.ShapeDtypeStruct((TP, 2, SLOT_ROWS, HEAD_SIZE), jnp.bfloat16),
            jax.ShapeDtypeStruct((2, 16, BLOCK_ROWS, HEAD_SIZE), jnp.bfloat16),
            jax.ShapeDtypeStruct((POOL, PAGE_POSITIONS, HEAD_SIZE), jnp.bfloat16),
            jax.ShapeDtypeStruct((4, PAGE_POSITIONS, HEAD_SIZE), jnp.bfloat16),
        ),
        in_specs=[vmem] * len(operands),
        out_specs=(vmem, vmem, pl.BlockSpec(memory_space=pl.ANY), vmem, vmem),
        scratch_shapes=[
            pltpu.VMEM((POOL, 64, HEAD_SIZE), jnp.bfloat16),
            pltpu.VMEM((KEY_VALUE_HEADS, 2, SLOT_ROWS, HEAD_SIZE), jnp.bfloat16),
            pltpu.VMEM((POOL, PAGE_POSITIONS, HEAD_SIZE), jnp.bfloat16),
            pltpu.VMEM((4, PAGE_POSITIONS, HEAD_SIZE), jnp.bfloat16),
            pltpu.VMEM((512, 512), jnp.bfloat16),
            dma((POOL,)),
            dma((POOL,)),
            dma((2, TP)),
            dma((2, TP)),
            dma((POOL,)),
            dma((POOL,)),
            dma((4,)),
            dma((4,)),
            dma((2, 4, 2)),
            dma((2, 4, 2)),
            dma,
            dma,
            dma((16,)),
            dma,
            dma,
        ],
        compiler_params=pltpu.CompilerParams(
            collective_id=0, has_side_effects=True, vmem_limit_bytes=VMEM_LIMIT
        ),
        name="fetch_and_prefill",
    )(*operands)


def decode_kernel(block_count, code, fresh_code, limit, cache_kv, gathered, result, rows, total, sem):
    load = pltpu.make_async_copy(
        gathered.at[:, :, pl.ds(WEIGHT_ROWS, QUERY_ROWS + FRESH_ROWS), :], rows, sem
    )
    load.start()
    total[...] = jnp.zeros_like(total)
    load.wait()
    queries = rows[:, :, :QUERY_ROWS].reshape(POOL * QUERY_ROWS, HEAD_SIZE)
    fresh = rows[:, :, QUERY_ROWS:].reshape(POOL * FRESH_ROWS, HEAD_SIZE)

    def one_block(i, carry):
        def picker(height, codes):
            at = lax.broadcasted_iota(jnp.int32, (height, 1), 0)
            wanted = (at // DECODE_BLOCK) * 256 + at % DECODE_BLOCK + i * DECODE_BLOCK
            same = codes == wanted.astype(jnp.float32)
            return jnp.where(same, 1.0, 0.0).astype(jnp.bfloat16)

        pick = picker(128, code[...])
        chosen = jnp.dot(pick, queries, preferred_element_type=jnp.float32)
        fresh_rows = jnp.dot(
            picker(64, fresh_code[...]), fresh, preferred_element_type=jnp.float32
        )
        scores = lax.dot_general(
            chosen.astype(jnp.bfloat16),
            cache_kv[:, 0].reshape(KEYS, HEAD_SIZE),
            NT,
            preferred_element_type=jnp.float32,
        )
        scores = jnp.where(limit[...] < DEAD, scores, -jnp.inf)
        top = jnp.max(scores, axis=1, keepdims=True)
        own_scores, own_values = [], []
        for step in range(DECODE_STEPS):
            keys = jnp.concatenate([fresh_rows[step * 32 : step * 32 + 16]] * 8, axis=0)
            own_values.append(
                jnp.concatenate([fresh_rows[step * 32 + 16 : step * 32 + 32]] * 8, axis=0)
            )
            score = jnp.sum(chosen * keys, axis=1, keepdims=True)
            if step == 1:
                at = lax.broadcasted_iota(jnp.int32, (128, 1), 0)
                score = jnp.where(at >= 64, score, -jnp.inf)
            own_scores.append(score)
            top = jnp.maximum(top, score)
        exponent = jnp.exp2(scores * EXP2_SCALE - top * EXP2_SCALE)
        mass = jnp.sum(exponent, axis=1, keepdims=True)
        mixed = jnp.dot(
            exponent.astype(jnp.bfloat16),
            cache_kv[:, 1].reshape(KEYS, HEAD_SIZE),
            preferred_element_type=jnp.float32,
        )
        for score, value in zip(own_scores, own_values):
            share = jnp.exp2(score * EXP2_SCALE - top * EXP2_SCALE)
            mass = mass + share
            mixed = mixed + share * value
        out = (mixed / mass).astype(jnp.bfloat16)
        total[...] += lax.dot_general(pick, out, TN, preferred_element_type=jnp.float32)
        return carry

    lax.fori_loop(0, block_count[0], one_block, 0)
    result[...] = total[...].astype(jnp.bfloat16)


def decode_call(*operands):
    vmem = pl.BlockSpec(memory_space=pltpu.VMEM)
    return pl.pallas_call(
        decode_kernel,
        out_shape=jax.ShapeDtypeStruct((POOL * QUERY_ROWS, HEAD_SIZE), jnp.bfloat16),
        in_specs=[pl.BlockSpec(memory_space=pltpu.SMEM)]
        + [vmem] * 4
        + [pl.BlockSpec(memory_space=pl.ANY)],
        out_specs=vmem,
        scratch_shapes=[
            pltpu.VMEM((2, 16, QUERY_ROWS + FRESH_ROWS, HEAD_SIZE), jnp.bfloat16),
            pltpu.VMEM((POOL * QUERY_ROWS, HEAD_SIZE), jnp.float32),
            pltpu.SemaphoreType.DMA,
        ],
        compiler_params=pltpu.CompilerParams(vmem_limit_bytes=VMEM_LIMIT),
        name="decode_rows",
    )(*operands)


CHUNKS = 4
CHUNK = 1024


def project_kernel(
    attention,
    decoded,
    gathered,
    out,
    decode_out,
    weight,
    partial,
    from_x,
    mid,
    from_y,
    from_pool,
    weight_sem,
    pool_send,
    pool_recv,
    x_send,
    x_recv,
    y_send,
    y_recv,
):
    me = lax.axis_index("pool")
    rank = lax.axis_index("tp")
    x = rank // 4
    y = rank % 4

    def weight_copy(chunk):
        places = pl.ds(chunk * 4, 4)
        return pltpu.make_async_copy(
            gathered.at[:, places, pl.ds(0, WEIGHT_ROWS), :],
            weight.at[:, places],
            weight_sem.at[chunk],
        )

    for chunk in range(CHUNKS):
        weight_copy(chunk).start()

    barrier = pltpu.get_barrier_semaphore()

    def greet_pool(i, carry):
        pl.semaphore_signal(
            barrier, inc=1, device_id={"pool": (me + i) % POOL}, device_id_type=MESH
        )
        return carry

    lax.fori_loop(1, POOL, greet_pool, 0)
    for i in range(1, 4):
        pl.semaphore_signal(
            barrier, inc=1, device_id={"tp": ((x + i) % 4) * 4 + y}, device_id_type=MESH
        )
        pl.semaphore_signal(
            barrier, inc=1, device_id={"tp": x * 4 + (y + i) % 4}, device_id_type=MESH
        )
    pl.semaphore_wait(barrier, POOL - 1 + 6)

    def pool_copy(i):
        to = (me + i) % POOL
        return remote(
            decoded.at[(to % 2) * 16 + to // 2],
            from_pool.at[i],
            pool_send.at[i],
            pool_recv.at[i],
            pool=to,
        )

    def x_copy(chunk, i):
        to = (x + i) % 4
        return remote(
            partial.at[chunk, pl.ds(to * 64, 64)],
            from_x.at[chunk, i],
            x_send.at[chunk, i],
            x_recv.at[chunk, i],
            tp=to * 4 + y,
        )

    def y_copy(chunk, i):
        to = (y + i) % 4
        return remote(
            mid.at[chunk, pl.ds(to * 16, 16)],
            from_y.at[chunk, i],
            y_send.at[chunk, i],
            y_recv.at[chunk, i],
            tp=x * 4 + to,
        )

    for chunk in range(CHUNKS):
        weight_copy(chunk).wait()

        def one_place(i, carry):
            for core in range(2):
                product = jnp.dot(
                    attention[...],
                    weight[core, chunk * 4 + i],
                    preferred_element_type=jnp.float32,
                )
                columns = pl.ds(pl.multiple_of(i * 256 + core * 128, 128), 128)
                partial[chunk, :, columns] = product.astype(jnp.bfloat16)
            return carry

        lax.fori_loop(0, 4, one_place, 0)
        for i in (2, 1, 3):
            x_copy(chunk, i).start()

    def start_pool(i, carry):
        pool_copy(i).start()
        return carry

    lax.fori_loop(1, POOL, start_pool, 0)
    from_pool[0] = decoded[(me % 2) * 16 + me // 2]

    for chunk in range(CHUNKS):
        for i in range(1, 4):
            x_copy(chunk, i).wait_recv()
        rows = partial[chunk, pl.ds(x * 64, 64), :].astype(jnp.float32)
        for i in range(1, 4):
            rows = rows + from_x[chunk, i].astype(jnp.float32)
        mid[chunk] = rows.astype(jnp.bfloat16)
        for i in range(1, 4):
            y_copy(chunk, i).start()

    def wait_pool(i, carry):
        pool_copy(i).wait()
        return carry

    lax.fori_loop(1, POOL, wait_pool, 0)

    def add_pool(i, carry):
        return carry + from_pool[i].astype(jnp.float32)

    decode_out[...] = lax.fori_loop(
        0, POOL, add_pool, jnp.zeros((QUERY_ROWS, HEAD_SIZE), jnp.float32)
    ).astype(jnp.bfloat16)

    for chunk in range(CHUNKS):
        for i in range(1, 4):
            y_copy(chunk, i).wait_recv()
        rows = mid[chunk, pl.ds(y * 16, 16), :].astype(jnp.float32)
        for i in range(1, 4):
            rows = rows + from_y[chunk, i].astype(jnp.float32)
        out[:, chunk * CHUNK : (chunk + 1) * CHUNK] = rows.astype(jnp.bfloat16)
    for chunk in range(CHUNKS):
        for i in range(1, 4):
            x_copy(chunk, i).wait_send()
            y_copy(chunk, i).wait_send()


def project_call(attention, decoded, gathered):
    vmem = pl.BlockSpec(memory_space=pltpu.VMEM)
    dma = pltpu.SemaphoreType.DMA
    return pl.pallas_call(
        project_kernel,
        out_shape=(
            jax.ShapeDtypeStruct((16, CHUNKS * CHUNK), jnp.bfloat16),
            jax.ShapeDtypeStruct((QUERY_ROWS, HEAD_SIZE), jnp.bfloat16),
        ),
        in_specs=[vmem, vmem, pl.BlockSpec(memory_space=pl.ANY)],
        out_specs=(vmem, vmem),
        scratch_shapes=[
            pltpu.VMEM((2, 16, WEIGHT_ROWS, HEAD_SIZE), jnp.bfloat16),
            pltpu.VMEM((CHUNKS, TURN_TOKENS, CHUNK), jnp.bfloat16),
            pltpu.VMEM((CHUNKS, 4, 64, CHUNK), jnp.bfloat16),
            pltpu.VMEM((CHUNKS, 64, CHUNK), jnp.bfloat16),
            pltpu.VMEM((CHUNKS, 4, 16, CHUNK), jnp.bfloat16),
            pltpu.VMEM((POOL, QUERY_ROWS, HEAD_SIZE), jnp.bfloat16),
            dma((CHUNKS,)),
            dma((POOL,)),
            dma((POOL,)),
            dma((CHUNKS, 4)),
            dma((CHUNKS, 4)),
            dma((CHUNKS, 4)),
            dma((CHUNKS, 4)),
        ],
        compiler_params=pltpu.CompilerParams(
            collective_id=1, has_side_effects=True, vmem_limit_bytes=VMEM_LIMIT
        ),
        name="project_and_return",
    )(attention, decoded, gathered)


def mixing_matrix():
    matrix = np.zeros((128, 128), np.float32)
    for head in range(8):
        for position in range(16):
            matrix[head * 16 + position, position * 8 + head] = 1
    return matrix


def page_codes():
    at = np.arange(512)
    return (((at % 128) // 4) * 16 + (at // 128) * 4 + at % 4).astype(np.float32)[None]


def per_device(
    turn_query_rows,
    turn_key_value,
    prefix_page_store,
    prefix_pages,
    holder_table,
    out_weight,
    row_request,
    step_query,
    step_kv,
):
    me = lax.axis_index("pool")
    rank = lax.axis_index("tp")
    store = prefix_page_store.reshape(POOL, 64, HEAD_SIZE)
    turn = turn_key_value.reshape(2, 128, HEAD_SIZE)
    queries = jnp.transpose(
        step_query.reshape(DECODE_STEPS, 8, HEADS_DEV, HEAD_SIZE), (0, 2, 1, 3)
    ).reshape(QUERY_ROWS, HEAD_SIZE)
    fresh = lax.dynamic_slice_in_dim(step_kv, (rank // 2) * HEAD_SIZE, HEAD_SIZE, 3)
    fresh = jnp.transpose(fresh, (0, 2, 1, 3)).reshape(FRESH_ROWS, HEAD_SIZE)
    block = jnp.concatenate([out_weight, queries, fresh], axis=0)

    holders = lax.dynamic_index_in_dim(holder_table, me, 0, keepdims=False)
    slot_of_page = (me - holders) % POOL
    live_pages = lax.dynamic_index_in_dim(prefix_pages, me, 0, keepdims=False)
    pages = jnp.arange(PREFIX_PAGE_CAP, dtype=jnp.int32)
    is_slot = slot_of_page[None, :] == pages[:, None]
    slot_live = jnp.any(is_slot & (pages[None, :] < live_pages), axis=1)
    slot_limit = jnp.where(slot_live, -1.0, DEAD)
    row = jnp.arange(SLOT_ROWS, dtype=jnp.int32)
    turn_position = jnp.arange(TP, dtype=jnp.float32)[:, None] * 16 + (row - 128)[None, :]
    limit = jnp.where(
        row[None, :] < 128, jnp.pad(jnp.repeat(slot_limit, 4), (0, 16))[None, :], turn_position
    ).reshape(1, KEYS)
    slot_for_target = jnp.roll(slot_of_page, me)
    row_code = (slot_for_target[:, None] * 16 + jnp.arange(16, dtype=jnp.int32)[None, :]).reshape(
        512, 1
    )

    attention, cache_kv, gathered, pages_in, turn_in = fetch_call(
        store,
        turn,
        block,
        turn_query_rows,
        limit,
        jnp.asarray(page_codes()),
        row_code.astype(jnp.float32),
        jnp.asarray(mixing_matrix(), jnp.bfloat16),
    )

    match = row_request == me
    row_ids = jnp.arange(256, dtype=jnp.int32)
    before = jnp.sum(
        jnp.where((row_ids[None, :] < row_ids[:, None]) & match[None, :], 1, 0), axis=1
    )
    block_count = (jnp.sum(match.astype(jnp.int32)) + DECODE_BLOCK - 1) // DECODE_BLOCK
    order = jnp.where(match, before, -10000).reshape(16, 2, 8)
    order = jnp.transpose(order, (1, 0, 2)).reshape(POOL, 1, 8)
    code = order + 256 * jnp.arange(8, dtype=jnp.int32)[None, :, None]
    fresh_code = order + 256 * jnp.arange(4, dtype=jnp.int32)[None, :, None]
    decoded = decode_call(
        block_count.reshape(1),
        code.reshape(1, POOL * QUERY_ROWS).astype(jnp.float32),
        fresh_code.reshape(1, POOL * FRESH_ROWS).astype(jnp.float32),
        limit,
        cache_kv,
        gathered,
    )
    prefill_out, decode_rows = project_call(
        attention, decoded.reshape(POOL, QUERY_ROWS, HEAD_SIZE), gathered
    )
    decode_out = jnp.transpose(
        decode_rows.reshape(DECODE_STEPS, HEADS_DEV, 8, HEAD_SIZE), (0, 2, 1, 3)
    ).reshape(DECODE_STEPS, 8, HEADS_DEV * HEAD_SIZE)

    slot = (me - pages) % POOL
    prefix_part = jnp.take(pages_in, slot, axis=0)
    turn_part = jnp.where(
        (slot < 4)[:, None, None], jnp.take(turn_in, jnp.minimum(slot, 3), axis=0), 0
    )
    both = jnp.stack([prefix_part, turn_part], axis=1)
    decode_cache = jnp.stack([both[..., :64], both[..., 64:]], axis=2)[None]
    return (prefill_out, decode_out, decode_cache)


def solution(mesh):
    placed = (
        P("pool", "tp"),
        P("pool", None, "tp", None),
        P("pool", None, "tp", None),
        P(),
        P(),
        P("tp", "pool"),
        P(),
        P(None, "pool", "tp"),
        P(None, "pool", None, None),
    )
    return jax.shard_map(
        per_device,
        mesh=mesh,
        in_specs=placed,
        out_specs=(
            P(("pool", "tp"), None),
            P(None, "pool", "tp"),
            P("pool", None, None, None, None, "tp"),
        ),
        check_vma=False,
    )
```

time: 520 us -> 163 us (0.31)
  Pallas kernels: 0 us -> 140 us
  waiting for transfers between devices: 128 us -> 0 us
  blocking collectives: 114 us -> 0 us
  starting transfers between devices: 83.9 us -> 0 us
  local copies, waits for them, and re-layouts: 84 us -> 12.3 us
  matrix products: 51.2 us -> 0 us
  other arithmetic: 39.5 us -> 6.28 us
  between operations: 14.6 us -> 1.56 us
    pallas_call x0 -> x3, Pallas kernels: none -> 140 us  [the longest x1 94.9 us: fetch_call(): pl.pallas_call(fetch_kernel, out_shape=(jax.ShapeDtypeStruct((TURN_TOKENS...]
    all_to_all x10 -> x0, waiting for transfers between devices: 127 us -> none  [the longest x1 37.6 us: per_device(): lax.all_to_all(outgoing, 'pool', split_axis=0, concat_axis=0, tiled=True)]
    all_gather x2 -> x0, blocking collectives: 114 us -> none  [per_device(): every_query = lax.all_gather(own_queries, 'pool', axis=0, tiled=True)]
    all_to_all x10 -> x0, starting transfers between devices: 83.9 us -> none  [the longest x2 21.9 us: per_device(): lax.all_to_all(top_score.reshape(pool_size, local_rows, heads_dev).astype...]
    dot_general x28 -> x0, matrix products: 51.2 us -> none  [the longest x10 25 us: partial_attention(): jnp.einsum('bkgd,bnkd->bkgn', query_rows, key_matrix, preferred_element_t...]
    gather x21 -> x2, local copies, waits for them, and re-layouts: 34.7 us -> 1.29 us  [the longest x1 0.65 us: per_device(): jnp.take(turn_in, jnp.minimum(slot, 3), axis=0)]
    slice x9 -> x0, local copies, waits for them, and re-layouts: 25.3 us -> none  [the longest x8 23.9 us: one_block(): gathered[:, :, 0]]
    select_n x22 -> x7, other arithmetic: 24.8 us -> 1.06 us  [the longest x1 0.7 us: per_device(): slot_of_page = (me - holders) % POOL]
  transfers between devices with their start and end apart: 12 -> 0, of which waited for: 8 -> 0; matrix products, arithmetic and copies ran while one was open for 33% -> 0% of each run, Pallas kernels for 0% -> 0%
where the time goes in v1:
time: 163 us; the launch traced here: 160 us
  Pallas kernels  140 us (86%)
  local copies, waits for them, and re-layouts  12.3 us (8%)
  other arithmetic  6.28 us (4%)
    pallas_call x1, Pallas kernels, fetch_call(): pl.pallas_call(fetch_kernel, out_shape=(jax.ShapeDtypeStruct((TURN_TOKENS...  94.9 us
    pallas_call x1, Pallas kernels, project_call(): pl.pallas_call(project_kernel, out_shape=(jax.ShapeDtypeStruct((16, CHUNK...  40.5 us
    pallas_call x1, Pallas kernels, decode_call(): pl.pallas_call(decode_kernel, out_shape=jax.ShapeDtypeStruct((POOL * QUER...  4.64 us

profile of v1, /device:TPU:7, one launch (start us, length us, event | category | flops | bytes accessed | tf_op | source)
XLA Modules:
  0.0 160.2 jit_solution(3649494274271899546)
XLA Ops:
  0.6 0.0 copy-start
  0.6 0.0 copy-start.5
  0.7 2.1 %reshape.309.store = bf16[32,64,128]{2,1,0:T(8,128)(2,1)} reshape(bf16[32,2,4,1024]{3,2,1,0:T(4,128)(2,1)} %param.13) | data formatting | bytes 1048576 | tf_op jit(solution)/shard_map/reshape | solution.py:690
  2.7 1.5 reshape.310.turn
  4.2 0.0 copy-done
  4.2 1.6 pad_maximum_fusion.1.block
  5.9 0.7 fusion.5
  6.6 1.2 dynamic_slice.17
  7.8 0.6 iota_compare_fusion.3
  8.5 0.1 fusion.4
  8.6 0.1 broadcast_in_dim.90
  8.7 0.1 reshape.314
  8.8 0.1 add_select_fusion
  8.9 0.7 select_n.159.limit
  9.6 0.7 and_select_fusion.2
  10.3 0.1 pad_add_fusion
  10.3 0.1 dynamic-slice_multiply_fusion
  10.4 0.1 add_convert_fusion.2
  10.5 0.9 convert_element_type.38.row_code
  11.4 94.9 %fetch_and_prefill.1 = (bf16[256,512]{1,0:T(8,128)(2,1)}, bf16[16,2,144,128]{3,2,1,0:T(8,128)(2,1)}, bf16[2,16,608,128]{3,2,1,0:T(8,128)(2,1)}, bf16[32,64,128]{2,1,0:T(8,128)(2,1)}, bf16[4,64,128]{2,1,0:T(8,128)(2,1)}) custom-call(bf16[32,64,128]{2,1,0:T(8,128)(2,1)} %reshape.309.store, bf16[2,128,128]{2,1,0:T(8,128)(2,1)} %reshape.310.turn, ...), custom_call_target="tpu_custom_call" | custom-call | tf_op jit(solution)/shard_map/fetch_and_prefill/pallas_call | solution.py:362
  106.3 0.0 copy-done.5
  106.3 0.6 convert_reduce_fusion
  107.6 0.1 select_reduce_fusion
  107.7 0.1 reshape.316
  107.9 0.1 add_convert_fusion
  107.9 0.7 convert_element_type.35.code
  108.7 0.1 add_convert_fusion.1
  108.7 0.7 convert_element_type.37.fresh_code
  109.5 4.6 %decode_rows.1 = bf16[2048,128]{1,0:T(8,128)(2,1)} custom-call(s32[1]{0:T(128)} %bitcast.8.block_count, f32[1,2048]{1,0:T(1,128)} %convert_element_type.35.code, f32[1,1024]{1,0:T(1,128)} %convert_element_type.37.fresh_code, f32[1,2304]{1,0:T(1,128)} %select_n.159.limit, bf16[16,2,144,128]{3,2,1,0:T(8,128)(2,1)} %get-tuple-element.11.cache_kv, ...), custom_call_target="tpu_custom_call" | custom-call | tf_op jit(solution)/shard_map/decode_rows/pallas_call | solution.py:465
  114.1 0.0 copy-start.1
  114.1 40.5 %project_and_return.1 = (bf16[16,4096]{1,0:T(8,128)(2,1)}, bf16[64,128]{1,0:T(8,128)(2,1)}) custom-call(bf16[256,512]{1,0:T(8,128)(2,1)} %get-tuple-element.10.attention, bf16[32,64,128]{2,1,0:T(8,128)(2,1)} %bitcast.40, bf16[2,16,608,128]{3,2,1,0:T(8,128)(2,1)} %get-tuple-element.12.gathered), custom_call_target="tpu_custom_call" | custom-call | tf_op jit(solution)/shard_map/project_and_return/pallas_call | solution.py:634
  154.6 0.0 copy-start.2
  154.6 0.0 copy-done.1
  154.6 0.6 gather_fusion.1
  155.3 0.1 fusion.1
  155.5 0.1 copy-done.2
  155.6 0.6 gather_fusion
  156.3 0.1 bitcast_select_fusion.1
  156.4 0.5 maximum_bitcast_fusion.1
  156.9 0.5 maximum_bitcast_fusion
  157.4 0.0 copy-start.3
  157.4 0.0 copy-start.4
  157.4 1.5 copy.30
  158.9 0.0 copy-done.3
  158.9 0.7 copy.35
  159.5 0.0 copy-done.4
  159.5 0.6 copy.36
  (16 shorter events, 0.1 us)
Async XLA Ops:
  0.6 3.6 %copy-start = (bf16[2,8,2,1024]{3,2,1,0:T(2,128)(2,1)S(1)}, bf16[2,8,2,1024]{3,2,1,0:T(2,128)(2,1)}, u32[]{:S(2)}) copy-start(bf16[2,8,2,1024]{3,2,1,0:T(2,128)(2,1)} %param.19) | copy-start | bytes 196612
  0.6 105.6 %copy-start.5 = (s32[256]{0:T(256)S(1)}, s32[256]{0:T(256)}, u32[]{:S(2)}) copy-start(s32[256]{0:T(256)} %param.17) | copy-start | bytes 3076
  114.1 40.5 %copy-start.1 = (bf16[4,64,128]{2,1,0:T(8,128)(2,1)S(1)}, bf16[4,64,128]{2,1,0:T(8,128)(2,1)}, u32[]{:S(2)}) copy-start(bf16[4,64,128]{2,1,0:T(8,128)(2,1)} %get-tuple-element.16) | copy-start | bytes 196612
  154.6 1.0 copy-start.2
  157.4 1.5 copy-start.3
  157.4 2.2 %copy-start.4 = (bf16[64,128]{1,0:T(8,128)(2,1)S(1)}, bf16[64,128]{1,0:T(8,128)(2,1)}, u32[]{:S(2)}) copy-start(bf16[64,128]{1,0:T(8,128)(2,1)} %get-tuple-element.14) | copy-start | bytes 49156
